TPU v7x, 32 devices: a whole 2x2x4 slice. The times are simulated.
32 devices in a mesh: groups: 2 (over y), seq: 4 (over z), head: 2 (over x), sub: 2 (over core).
Axes of the slice: x: 2, y: 2, z: 4, core: 2. Of those that a mesh axis runs over, the one named last changes fastest.
Arguments:
- hidden: bfloat16 [4096, 5376], P(('groups', 'seq'), 'sub'), parts along dimension 0, may hold values from -500 to 500
- norm_gain: float32 [5376], replicated, may hold values from 0.25 to 1.75
- w_query: bfloat16 [5376, 4096], P('seq', ('head', 'sub')), may hold values from -0.078125 to 0.078125
- w_key: bfloat16 [5376, 2048], P('seq', ('head', 'sub')), may hold values from -0.078125 to 0.078125
- w_value: bfloat16 [5376, 2048], P('seq', ('head', 'sub')), may hold values from -0.078125 to 0.078125
- query_gain: float32 [128], replicated, may hold values from 1 to 2.5
- key_gain: float32 [128], replicated, may hold values from 1 to 2.5
- block_source: int32 [32], P('groups'), parts along dimension 0, may hold values from 0 to 15, as said below
- block_doc: int32 [32], P('groups'), parts along dimension 0, may hold values from 0 to 3, never falling along the last dimension, each value on 1 to 8 neighbouring positions
Outputs:
- attention: bfloat16 [4096, 4096], P(('groups', 'seq'), ('head', 'sub')), parts along dimension 0
There are 2 independent parts, one for each index of `groups`. A program takes and returns all parts, laid end to end along the dimension named above; an argument that names none is the same for every part. Nothing has to cross between parts.
Inputs may be any that keep to these rules, and one draw needn't show every extreme that they name: block_source[b] is the arrival slot of block b, rows block_source[b] * 128 to block_source[b] * 128 + 127 of hidden, on shard block_source[b] // 4; each slot holds one block. Block b lies on its own shard b // 4 or on the shard just before or just after it. Of one shard's blocks at most 2 lie on each neighbouring shard, exactly as many as that neighbour's blocks lie on it, and in every draw some shard holds exactly 2 blocks of each of its two neighbours. `block_doc`: document ids never fall along the blocks; each document spans 1 to 8 blocks, one exactly 8.
All inputs are finite; a program needn't handle non-finite values.
Results may differ from a plain program's by a relative error of at most 0.012.
Values may be sent and summed in bfloat16 or wider, within the bound.
A program may use at most 128 MiB of HBM per device.

v0:
```python
import jax
import jax.numpy as jnp
from jax import lax
from jax.sharding import PartitionSpec as P

HEAD_DIM = 128
WINDOW = 1024
BLOCK = 128
CAP = 2
QUERY_SCALE = 168.0 ** (-0.5)
EPSILON = 1e-06
ROPE_BASE = 10000.0


def passed_along(x, axis, by):
    size = lax.axis_size(axis)
    pairs = [(i, i + by) for i in range(size) if 0 <= i + by < size]
    return lax.ppermute(x, axis, pairs)


def table_lookup(table, indices):
    hits = indices[:, None] == jnp.arange(table.shape[0], dtype=jnp.int32)[None, :]
    return jnp.sum(jnp.where(hits, table[None, :], 0), axis=1)


def token_positions(block_ids, block_doc):
    first_block = jnp.sum((block_doc[None, :] < block_doc[:, None]).astype(jnp.int32), axis=1)
    start_block = table_lookup(first_block, block_ids)
    within = jnp.arange(BLOCK, dtype=jnp.int32)
    return (
        ((block_ids - start_block)[:, None] * BLOCK + within[None, :])
        .reshape(-1)
        .astype(jnp.float32)
    )


def token_docs(token_ids, block_doc):
    return table_lookup(block_doc, jnp.floor_divide(token_ids, BLOCK))


def head_rotation(values, gain, positions, factor):
    token_count = values.shape[0]
    per_head = values.reshape(token_count, -1, HEAD_DIM)
    normed = (
        per_head * lax.rsqrt(jnp.mean(per_head * per_head, axis=2, keepdims=True) + EPSILON) * gain
    )
    half_dim = HEAD_DIM // 2
    frequency = ROPE_BASE ** (-(jnp.arange(half_dim, dtype=jnp.float32) * 2.0 / HEAD_DIM))
    angles = positions[:, None] * frequency[None, :]
    cosine = jnp.cos(angles)[:, None, :]
    sine_table = jnp.sin(angles)[:, None, :]
    first_half = normed[:, :, :half_dim]
    second_half = normed[:, :, half_dim:]
    turned = jnp.concatenate(
        [
            first_half * cosine - second_half * sine_table,
            second_half * cosine + first_half * sine_table,
        ],
        axis=2,
    )
    return (turned * factor).reshape(token_count, -1).astype(jnp.bfloat16)


def side_ranks(labels):
    length = labels.shape[0]
    earlier = jnp.arange(length)[None, :] < jnp.arange(length)[:, None]
    matching = labels[None, :] == labels[:, None]
    return jnp.sum((earlier & matching).astype(jnp.int32), axis=1)


def outgoing_slots(block_source, target, own_shard, block_count, shard_count):
    first_slot = jnp.clip(target, 0, shard_count - 1) * block_count
    slot_ids = lax.dynamic_slice_in_dim(block_source, first_slot, block_count)
    sending = (slot_ids // block_count == own_shard) & (target >= 0) & (target < shard_count)
    send_rank = side_ranks(sending.astype(jnp.int32))
    wanted = (jnp.arange(CAP)[:, None] == send_rank[None, :]) & sending[None, :]
    return jnp.sum(jnp.where(wanted, (slot_ids % block_count)[None, :], 0), axis=1)


def incoming_index(block_source, own_shard, block_count):
    slot_ids = lax.dynamic_slice_in_dim(block_source, own_shard * block_count, block_count)
    sides = slot_ids // block_count - own_shard
    side_rank = side_ranks(sides)
    from_prior = block_count + side_rank
    from_next = block_count + CAP + side_rank
    return jnp.where(
        sides == 0, slot_ids % block_count, jnp.where(sides < 0, from_prior, from_next)
    )


def migrate(values, block_source, own_shard, shard_count):
    row_count, col_count = values.shape
    block_count = row_count // BLOCK
    pieces = values.reshape(block_count, BLOCK, col_count)
    block_pool = [pieces]
    for offset in (1, -1):
        chosen = outgoing_slots(
            block_source, own_shard + offset, own_shard, block_count, shard_count
        )
        outgoing = jnp.take(pieces, chosen, axis=0)
        block_pool.append(passed_along(outgoing, "seq", offset))
    joined = jnp.concatenate(block_pool, axis=0)
    placed = jnp.take(joined, incoming_index(block_source, own_shard, block_count), axis=0)
    return placed.reshape(row_count, col_count)


def project_rows(halves, norm_gain, w_query, w_key, w_value, query_gain, key_gain, positions):
    full_rows = lax.all_gather(halves, "sub", axis=1, tiled=True)
    as_float = full_rows.astype(jnp.float32)
    normed = (
        as_float
        * lax.rsqrt(jnp.mean(as_float * as_float, axis=1, keepdims=True) + EPSILON)
        * norm_gain
    ).astype(jnp.bfloat16)
    segments = (
        lax.all_gather(w_query, "seq", axis=0, tiled=True),
        lax.all_gather(w_key, "seq", axis=0, tiled=True),
        lax.all_gather(w_value, "seq", axis=0, tiled=True),
    )
    query_raw, key_raw, value_raw = tuple(
        (jnp.dot(normed, segment, preferred_element_type=jnp.float32) for segment in segments)
    )
    query_rot = head_rotation(query_raw, query_gain, positions, QUERY_SCALE)
    key_rot = head_rotation(key_raw, key_gain, positions, 1.0)
    return jnp.concatenate([query_rot, key_rot, value_raw.astype(jnp.bfloat16)], axis=1)


def attend_block(query_rows, key_rows, value_rows, query_tokens, key_tokens, query_docs, key_docs):
    query_count = query_rows.shape[0]
    key_count = key_rows.shape[0]
    kv_count = key_rows.shape[1] // HEAD_DIM
    query_heads = query_rows.reshape(query_count, kv_count, 2, HEAD_DIM)
    key_heads = key_rows.reshape(key_count, kv_count, HEAD_DIM)
    value_heads = value_rows.reshape(key_count, kv_count, HEAD_DIM)
    scores = jnp.einsum(
        "qgjd,kgd->gjqk", query_heads, key_heads, preferred_element_type=jnp.float32
    )
    allowed = (key_tokens[None, :] >= 0) & (key_tokens[None, :] <= query_tokens[:, None])
    allowed = (
        allowed
        & (query_tokens[:, None] - key_tokens[None, :] < WINDOW)
        & (key_docs[None, :] == query_docs[:, None])
    )
    weight_exp = jnp.where(allowed, jnp.exp(scores), 0.0)
    totals = jnp.sum(weight_exp, axis=3)
    summed = jnp.einsum(
        "gjqk,kgd->qgjd",
        weight_exp.astype(jnp.bfloat16),
        value_heads,
        preferred_element_type=jnp.float32,
    )
    return (
        (summed / jnp.transpose(totals, (2, 0, 1))[:, :, :, None])
        .reshape(query_count, -1)
        .astype(jnp.bfloat16)
    )


def body(hidden, norm_gain, w_query, w_key, w_value, query_gain, key_gain, block_source, block_doc):
    row_count = hidden.shape[0]
    block_count = row_count // BLOCK
    own_shard = lax.axis_index("seq")
    shard_count = lax.axis_size("seq")
    own_blocks = own_shard * block_count + jnp.arange(block_count, dtype=jnp.int32)
    moved = migrate(hidden, block_source, own_shard, shard_count)
    packed = project_rows(
        moved,
        norm_gain,
        w_query,
        w_key,
        w_value,
        query_gain,
        key_gain,
        token_positions(own_blocks, block_doc),
    )
    query_width = w_query.shape[1]
    key_width = w_key.shape[1]
    query_rot = packed[:, :query_width]
    key_value = packed[:, query_width:]
    halo_count = max(1, WINDOW // row_count)
    received = []
    for distance in range(halo_count, 0, -1):
        received.append(passed_along(key_value, "seq", distance))
    extended = jnp.concatenate(received + [key_value], axis=0)
    key_all = extended[:, :key_width]
    value_all = extended[:, key_width:]
    query_tokens = own_shard * row_count + jnp.arange(row_count, dtype=jnp.int32)
    key_tokens = own_shard * row_count - WINDOW + jnp.arange(extended.shape[0], dtype=jnp.int32)
    query_docs = token_docs(query_tokens, block_doc)
    key_docs = token_docs(key_tokens, block_doc)
    block_rows = min(512, row_count)

    def one_block(block_index):
        return attend_block(
            query_rot, key_all, value_all, query_tokens, key_tokens, query_docs, key_docs
        )

    result = lax.map(one_block, jnp.arange(row_count // block_rows, dtype=jnp.int32))
    return result.reshape(row_count, -1)


def solution(mesh):
    placed = (
        P(("groups", "seq"), "sub"),
        P(),
        P("seq", ("head", "sub")),
        P("seq", ("head", "sub")),
        P("seq", ("head", "sub")),
        P(),
        P(),
        P("groups"),
        P("groups"),
    )
    return jax.shard_map(
        body,
        mesh=mesh,
        in_specs=placed,
        out_specs=P(("groups", "seq"), ("head", "sub")),
        check_vma=False,
    )
```

profile of v0, /device:TPU:25, one launch (start us, length us, event | category | flops | bytes accessed | tf_op | source)
XLA Modules:
  0.0 590.2 jit_solution(7441517687041226296)
XLA Ops:
  6.5 0.9 fusion.27
  7.5 0.2 convert_reduce_fusion.3
  7.6 0.9 compare_and_fusion.2
  8.5 0.2 convert_reduce_fusion.2
  8.7 0.2 convert_reduce_fusion.1
  9.1 3.5 gather_fusion.2
  12.6 2.6 broadcast_select_fusion
  15.2 3.2 collective-permute-start.1
  18.5 1.8 gather_fusion.1
  20.3 1.5 broadcast_select_fusion.1
  21.8 1.3 collective-permute-start
  23.2 23.3 %collective-permute-done.1 = bf16[2,128,2688]{2,1,0:T(8,128)(2,1)} collective-permute-done((bf16[2,128,2688]{2,1,0:T(8,128)(2,1)}, bf16[2,128,2688]{2,1,0:T(8,128)(2,1)}, u32[]{:S(2)}, u32[]{:S(2)}) %collective-permute-start.1) | collective-permute-done | bytes 1376288 | tf_op jit(solution)/shard_map/ppermute | solution.py:18
  46.5 8.0 %collective-permute-done = bf16[2,128,2688]{2,1,0:T(8,128)(2,1)S(1)} collective-permute-done((bf16[2,128,2688]{2,1,0:T(8,128)(2,1)S(1)}, bf16[2,128,2688]{2,1,0:T(8,128)(2,1)S(1)}, u32[]{:S(2)}, u32[]{:S(2)}) %collective-permute-start) | collective-permute-done | bytes 1376288 | tf_op jit(solution)/shard_map/ppermute | solution.py:18
  54.4 4.2 pad_maximum_fusion
  58.6 3.5 gather_fusion
  62.1 2.2 bitcast_select_fusion.1
  64.4 0.7 all-gather.7.cloned.1.call-update
  65.2 0.7 all-gather.9.cloned.1.call-update
  65.9 0.5 all-gather.11.cloned.1.call-update
  66.5 0.2 convert_reduce_fusion
  66.6 0.2 select_reduce_fusion.2
  66.9 1.0 multiply_cosine_fusion
  68.2 14.8 %all-gather.5.cloned.1.call-done = bf16[512,5376]{1,0:T(8,128)(2,1)} async-done(((bf16[512,2688]{1,0:T(8,128)(2,1)}), bf16[512,5376]{1,0:T(8,128)(2,1)}) %all-gather.5.cloned.1.call-update) | async-done | bytes 5505040 | tf_op jit(solution)/shard_map/all_gather | solution.py:108
  83.0 3.7 fusion.6
  86.7 98.0 %all-gather.7.cloned.1.call-done = bf16[5376,512]{1,0:T(8,128)(2,1)} async-done(((bf16[1344,512]{1,0:T(8,128)(2,1)}), bf16[5376,512]{1,0:T(8,128)(2,1)}) %all-gather.7.cloned.1.call-update) | async-done | bytes 5505040 | tf_op jit(solution)/shard_map/all_gather | solution.py:117
  184.7 8.0 %multiply_reduce_fusion.1 = (f32[512,4]{0,1:T(4,128)S(1)}, f32[512,512]{0,1:T(8,128)S(1)}) fusion(bf16[5376,512]{1,0:T(8,128)(2,1)} %all-gather.7.cloned.1.call-done, bf16[512,5376]{1,0:T(8,128)(2,1)} %all-gather.5.cloned.1.call-done, f32[5376]{0:T(1024)S(1)} %copy-done.7, f32[512]{0:T(512)S(1)} %add_rsqrt_fusion.2), kind=kOutput, calls=%fused_computation.34 | convolution fusion | flops 2830104576 | bytes 12090368 | tf_op jit(solution)/shard_map/dot_general | solution.py:121
  192.8 0.2 multiply_multiply_fusion.1
  193.2 93.9 %all-gather.9.cloned.1.call-done = bf16[5376,512]{1,0:T(8,128)(2,1)} async-done(((bf16[1344,512]{1,0:T(8,128)(2,1)}), bf16[5376,512]{1,0:T(8,128)(2,1)}) %all-gather.9.cloned.1.call-update) | async-done | bytes 5505040 | tf_op jit(solution)/shard_map/all_gather | solution.py:118
  287.0 7.4 %convolution_convert_fusion = bf16[512,512]{0,1:T(8,128)(2,1)S(1)} fusion(bf16[5376,512]{1,0:T(8,128)(2,1)} %all-gather.9.cloned.1.call-done, bf16[512,5376]{1,0:T(8,128)(2,1)} %all-gather.5.cloned.1.call-done, f32[5376]{0:T(1024)S(1)} %copy-done.7, f32[512]{0:T(512)S(1)} %add_rsqrt_fusion.2), kind=kOutput, calls=%fused_computation.31 | convolution fusion | flops 2829844480 | bytes 11557888 | tf_op jit(solution)/shard_map/dot_general | solution.py:121
  294.5 1.3 collective-permute-start.3
  295.8 1.5 collective-permute-start.2
  297.5 2.6 fusion.10
  300.1 55.7 %collective-permute-done.3 = bf16[512,1024]{0,1:T(8,128)(2,1)S(1)} collective-permute-done((bf16[512,1024]{0,1:T(8,128)(2,1)S(1)}, bf16[512,1024]{0,1:T(8,128)(2,1)S(1)}, u32[]{:S(2)}, u32[]{:S(2)}) %collective-permute-start.3) | collective-permute-done | bytes 1048608 | tf_op jit(solution)/shard_map/ppermute | solution.py:18
  355.8 118.7 %collective-permute-done.2 = bf16[512,1024]{0,1:T(8,128)(2,1)S(1)} collective-permute-done((bf16[512,1024]{0,1:T(8,128)(2,1)S(1)}, bf16[512,1024]{0,1:T(8,128)(2,1)S(1)}, u32[]{:S(2)}, u32[]{:S(2)}) %collective-permute-start.2) | collective-permute-done | bytes 1048608 | tf_op jit(solution)/shard_map/ppermute | solution.py:18
  474.5 9.2 %maximum_maximum_fusion = bf16[1536,1024]{0,1:T(8,128)(2,1)S(1)} fusion(bf16[512,512]{0,1:T(8,128)(2,1)S(1)} %convolution_convert_fusion, bf16[512,512]{0,1:T(8,128)(2,1)S(1)} %bitcast.52, bf16[512,1024]{0,1:T(8,128)(2,1)S(1)} %collective-permute-done.3, bf16[512,1024]{0,1:T(8,128)(2,1)S(1)} %collective-permute-done.2), kind=kLoop, calls=%fused_computation.15 | loop fusion | flops 12582912 | bytes 6291456 | tf_op jit(solution)/shard_map/concatenate | solution.py:184
  483.6 1.9 fusion.35
  485.6 59.4 %all-gather.11.cloned.1.call-done = bf16[5376,1024]{1,0:T(8,128)(2,1)} async-done(((bf16[1344,1024]{1,0:T(8,128)(2,1)}), bf16[5376,1024]{1,0:T(8,128)(2,1)}) %all-gather.11.cloned.1.call-update) | async-done | bytes 11010064 | tf_op jit(solution)/shard_map/all_gather | solution.py:116
  545.0 10.3 %convolution_bitcast_fusion = f32[64,8,8,128]{3,1,2,0:T(8,128)S(1)} fusion(bf16[5376,1024]{1,0:T(8,128)(2,1)} %all-gather.11.cloned.1.call-done, bf16[512,5376]{1,0:T(8,128)(2,1)} %all-gather.5.cloned.1.call-done, f32[5376]{0:T(1024)S(1)} %copy-done.7, f32[512]{0:T(512)S(1)} %add_rsqrt_fusion.2), kind=kOutput, calls=%fused_computation.28 | convolution fusion | flops 5648154624 | bytes 18635776 | tf_op jit(solution)/shard_map/dot_general | solution.py:121
  555.3 0.5 copy.42
  555.8 0.6 multiply_reduce_fusion
  556.7 0.9 multiply_multiply_fusion
  557.5 1.1 multiply_subtract_fusion
  558.7 0.6 fusion.11
  559.4 0.6 copy-done.2
  560.1 0.2 copy-done.3
  560.3 11.3 %fusion = (f32[4,2,512]{2,1,0:T(2,128)S(1)}, f32[4,1536,512,2]{2,1,3,0:T(8,128)}) fusion(pred[512,1536]{0,1:T(8,128)(4,1)S(1)} %copy-done.3, bf16[1536,4,128,1]{0,2,3,1:T(8,128)(2,1)S(1)} %bitcast.54, bf16[512,4,2,128]{3,0,2,1:T(8,128)(2,1)S(1)} %bitcast.55), kind=kOutput, calls=%fused_computation.4 | convolution fusion | flops 1623191552 | bytes 28590080 | tf_op jit(solution)/shard_map/while/body/eval_jaxpr/qgjd,kgd->gjqk/dot_general | solution.py:135
  571.6 10.7 %fusion.12 = bf16[512,4,2,128]{0,3,2,1:T(8,128)(2,1)S(1)} fusion(bf16[1536,4,128,1]{0,2,3,1:T(8,128)(2,1)S(1)} %bitcast.53, f32[4,1536,512,2]{2,1,3,0:T(8,128)} %get-tuple-element.57, pred[512,1536]{0,1:T(8,128)(4,1)S(1)} %copy-done.3, f32[512,4,2]{0,2,1:T(2,128)S(1)} %bitcast.57), kind=kOutput, calls=%fused_computation.23 | convolution fusion | flops 1624244224 | bytes 28590080 | tf_op jit(solution)/shard_map/while/body/eval_jaxpr/gjqk,kgd->qgjd/dot_general | solution.py:146
  582.3 1.3 copy.36
  (48 shorter events, 1.6 us)
Async XLA Ops:
  6.5 11.9 %copy-start = (bf16[512,2688]{1,0:T(8,128)(2,1)S(1)}, bf16[512,2688]{1,0:T(8,128)(2,1)}, u32[]{:S(2)}) copy-start(bf16[512,2688]{1,0:T(8,128)(2,1)} %param.11) | copy-start | bytes 8257540
  6.5 76.4 %all-gather.5.cloned.1.call-start = ((), (), s32[]{:S(2)}) async-start(), calls=%async_computation | async-start | bytes 8257536 | tf_op jit(solution)/shard_map/all_gather | solution.py:108
  15.2 31.2 %collective-permute-start.1 = (bf16[2,128,2688]{2,1,0:T(8,128)(2,1)}, bf16[2,128,2688]{2,1,0:T(8,128)(2,1)}, u32[]{:S(2)}, u32[]{:S(2)}) collective-permute-start(bf16[2,128,2688]{2,1,0:T(8,128)(2,1)} %broadcast_select_fusion), channel_id=1, source_target_pairs={{4,0},{8,4},{12,8},{5,1},{9,5},{13,9},{6,2},{10,6},{14,10},{7,3},{... | collective-permute-start | bytes 4128776 | tf_op jit(solution)/shard_map/ppermute | solution.py:18
  21.8 32.6 %collective-permute-start = (bf16[2,128,2688]{2,1,0:T(8,128)(2,1)S(1)}, bf16[2,128,2688]{2,1,0:T(8,128)(2,1)S(1)}, u32[]{:S(2)}, u32[]{:S(2)}) collective-permute-start(bf16[2,128,2688]{2,1,0:T(8,128)(2,1)S(1)} %broadcast_select_fusion.1), channel_id=1, source_target_pairs={{0,4},{4,8},{8,12},{1,5},{5,9},{9,13},{2,6},{6,10},{10,14},{3,7},{... | collective-permute-start | bytes 4128776 | tf_op jit(solution)/shard_map/ppermute | solution.py:18
  64.4 2.1 copy-start.4
  64.4 120.3 %all-gather.7.cloned.1.call-start = ((), (), s32[]{:S(2)}) async-start(), calls=%async_computation.1 | async-start | bytes 6881280 | tf_op jit(solution)/shard_map/all_gather | solution.py:117
  65.1 221.9 %all-gather.9.cloned.1.call-start = ((), (), s32[]{:S(2)}) async-start(), calls=%async_computation.2 | async-start | bytes 6881280 | tf_op jit(solution)/shard_map/all_gather | solution.py:118
  65.9 479.1 %all-gather.11.cloned.1.call-start = ((), (), s32[]{:S(2)}) async-start(), calls=%async_computation.3 | async-start | bytes 13762560 | tf_op jit(solution)/shard_map/all_gather | solution.py:116
  67.9 116.8 %copy-start.7 = (f32[5376]{0:T(1024)S(1)}, f32[5376]{0:T(1024)}, u32[]{:S(2)}) copy-start(f32[5376]{0:T(1024)} %param.12) | copy-start | bytes 64516
  86.7 106.0 %copy-start.5 = (f32[128]{0:T(128)S(1)}, f32[128]{0:T(128)}, u32[]{:S(2)}) copy-start(f32[128]{0:T(128)} %param.17) | copy-start | bytes 1540
  294.5 61.3 %collective-permute-start.3 = (bf16[512,1024]{0,1:T(8,128)(2,1)S(1)}, bf16[512,1024]{0,1:T(8,128)(2,1)S(1)}, u32[]{:S(2)}, u32[]{:S(2)}) collective-permute-start(bf16[512,1024]{0,1:T(8,128)(2,1)S(1)} %pad_maximum_fusion.1), channel_id=1, source_target_pairs={{0,4},{4,8},{8,12},{1,5},{5,9},{9,13},{2,6},{6,10},{10,14},{3,7},{... | collective-permute-start | bytes 3145736 | tf_op jit(solution)/shard_map/ppermute | solution.py:18
  295.8 178.7 %collective-permute-start.2 = (bf16[512,1024]{0,1:T(8,128)(2,1)S(1)}, bf16[512,1024]{0,1:T(8,128)(2,1)S(1)}, u32[]{:S(2)}, u32[]{:S(2)}) collective-permute-start(bf16[512,1024]{0,1:T(8,128)(2,1)S(1)} %pad_maximum_fusion.1), channel_id=1, source_target_pairs={{0,8},{4,12},{1,9},{5,13},{2,10},{6,14},{3,11},{7,15},{16,24},{20,... | collective-permute-start | bytes 3145736 | tf_op jit(solution)/shard_map/ppermute | solution.py:18
  555.3 1.4 copy-start.6
  558.6 1.4 copy-start.2
  558.7 1.6 copy-start.3
  560.3 11.3 %copy-start.1 = (bf16[1536,512]{0,1:T(8,128)(2,1)S(1)}, bf16[1536,512]{0,1:T(8,128)(2,1)}, u32[]{:S(2)}) copy-start(bf16[1536,512]{0,1:T(8,128)(2,1)} %get-tuple-element.40) | copy-start | bytes 4718596
Sparse Core Ops, SparseCore 0:
  64.5 18.4 all-gather.4
  84.5 100.1 all-gather.6
  186.3 100.7 all-gather.8
  288.5 256.4 all-gather.10
where the time goes:
time: 591 us; the launch traced here: 590 us
  waiting for transfers between devices  474 us (80%)
  matrix products  47.7 us (8%)
  other arithmetic  33.9 us (6%)
  local copies, waits for them, and re-layouts  14 us (2%)
  between operations  13.5 us (2%)
  starting transfers between devices  7.37 us (1%)
    ppermute x4, waiting for transfers between devices, passed_along(): return lax.ppermute(x, axis, pairs)  206 us
    all_gather x1, waiting for transfers between devices, project_rows(): lax.all_gather(w_key, 'seq', axis=0, tiled=True)  98 us
    all_gather x1, waiting for transfers between devices, project_rows(): lax.all_gather(w_value, 'seq', axis=0, tiled=True)  93.9 us
    all_gather x1, waiting for transfers between devices, project_rows(): lax.all_gather(w_query, 'seq', axis=0, tiled=True)  59.4 us
    dot_general x3, matrix products, project_rows(): jnp.dot(normed, segment, preferred_element_type=jnp.float32)  25.7 us
    all_gather x1, waiting for transfers between devices, project_rows(): full_rows = lax.all_gather(halves, 'sub', axis=1, tiled=True)  14.8 us
  transfers between devices with their start and end apart: 8, of which 8 were waited for; matrix products, arithmetic and copies ran while one was open for 7% of the time, Pallas kernels for 0%

commit v1 on v0

--- a/solution.py
+++ b/solution.py
@@ -10,6 +10,27 @@
 QUERY_SCALE = 168.0 ** (-0.5)
 EPSILON = 1e-06
 ROPE_BASE = 10000.0
+
+
+def collect(x, axis, dim):
+    size, place, rows = (lax.axis_size(axis), lax.axis_index(axis), x.shape[dim])
+    upward = [(i, (i + 1) % size) for i in range(size)]
+    behind = [(i, (i - 1) % size) for i in range(size)]
+    out = jnp.zeros((*x.shape[:dim], size * rows, *x.shape[dim + 1 :]), x.dtype)
+    out = lax.dynamic_update_slice_in_dim(out, x, place * rows, axis=dim)
+    from_left = from_right = x
+    halfway = size // 2
+    for turn in range(1, halfway + 1):
+        from_left = lax.ppermute(from_left, axis, upward)
+        out = lax.dynamic_update_slice_in_dim(
+            out, from_left, (place - turn) % size * rows, axis=dim
+        )
+        if turn < size - halfway:
+            from_right = lax.ppermute(from_right, axis, behind)
+            out = lax.dynamic_update_slice_in_dim(
+                out, from_right, (place + turn) % size * rows, axis=dim
+            )
+    return out
 
 
 def passed_along(x, axis, by):
@@ -114,7 +135,7 @@
     ).astype(jnp.bfloat16)
     segments = (
         lax.all_gather(w_query, "seq", axis=0, tiled=True),
-        lax.all_gather(w_key, "seq", axis=0, tiled=True),
+        collect(w_key, "seq", 0),
         lax.all_gather(w_value, "seq", axis=0, tiled=True),
     )
     query_raw, key_raw, value_raw = tuple(

time: 591 us -> 548 us (0.927)
  waiting for transfers between devices: 474 us -> 419 us
  local copies, waits for them, and re-layouts: 14 us -> 25.9 us
    ppermute x0 -> x3, waiting for transfers between devices: none -> 137 us  [the longest x2 89.3 us: collect(): from_left = lax.ppermute(from_left, axis, upward)]
    all_gather x1 -> x0, waiting for transfers between devices: 98 us -> none  [project_rows(): lax.all_gather(w_key, 'seq', axis=0, tiled=True)]
    all_gather x1, waiting for transfers between devices: 93.9 us -> 16.6 us  [project_rows(): lax.all_gather(w_value, 'seq', axis=0, tiled=True)]
    all_gather x1, waiting for transfers between devices: 14.8 us -> 0.01 us  [project_rows(): full_rows = lax.all_gather(halves, 'sub', axis=1, tiled=True)]
    dynamic_update_slice x0 -> x4, local copies, waits for them, and re-layouts: none -> 8.81 us  [the longest x2 5.09 us: collect(): lax.dynamic_update_slice_in_dim(out, from_left, (place - turn) % size * r...]
  transfers between devices with their start and end apart: 8 -> 10, of which waited for: 8 -> 9; matrix products, arithmetic and copies ran while one was open for 7% -> 9% of each run, Pallas kernels for 0% -> 0%
where the time goes in v1:
time: 548 us
  waiting for transfers between devices  419 us (76%)
  matrix products  45.6 us (8%)
  other arithmetic  34.1 us (6%)
  local copies, waits for them, and re-layouts  25.9 us (5%)
  between operations  13.5 us (2%)
  starting transfers between devices  10.2 us (2%)
    ppermute x4, waiting for transfers between devices, passed_along(): return lax.ppermute(x, axis, pairs)  204 us
    ppermute x2, waiting for transfers between devices, collect(): from_left = lax.ppermute(from_left, axis, upward)  89.3 us
    all_gather x1, waiting for transfers between devices, project_rows(): lax.all_gather(w_query, 'seq', axis=0, tiled=True)  60 us
    ppermute x1, waiting for transfers between devices, collect(): from_right = lax.ppermute(from_right, axis, behind)  47.4 us
    dot_general x3, matrix products, project_rows(): jnp.dot(normed, segment, preferred_element_type=jnp.float32)  23.5 us
    all_gather x1, waiting for transfers between devices, project_rows(): lax.all_gather(w_value, 'seq', axis=0, tiled=True)  16.6 us
    dot_general x1, matrix products, attend_block(): jnp.einsum('qgjd,kgd->gjqk', query_heads, key_heads, preferred_element_ty...  11.4 us
  transfers between devices with their start and end apart: 10, of which 9 were waited for; matrix products, arithmetic and copies ran while one was open for 9% of the time, Pallas kernels for 0%

profile of v1, /device:TPU:25, one launch (start us, length us, event | category | flops | bytes accessed | tf_op | source)
XLA Modules:
  0.0 547.9 jit_solution(1554839180911790925)
XLA Ops:
  6.5 0.9 fusion.27
  7.6 0.9 compare_and_fusion.2
  9.1 3.5 gather_fusion.2
  12.6 2.6 broadcast_select_fusion
  15.2 3.2 collective-permute-start.1
  18.5 1.8 gather_fusion.1
  20.3 1.5 broadcast_select_fusion.1
  21.8 1.3 collective-permute-start
  23.2 23.3 %collective-permute-done.1 = bf16[2,128,2688]{2,1,0:T(8,128)(2,1)} collective-permute-done((bf16[2,128,2688]{2,1,0:T(8,128)(2,1)}, bf16[2,128,2688]{2,1,0:T(8,128)(2,1)}, u32[]{:S(2)}, u32[]{:S(2)}) %collective-permute-start.1) | collective-permute-done | bytes 1376288 | tf_op jit(solution)/shard_map/ppermute | solution.py:39
  46.5 8.0 %collective-permute-done = bf16[2,128,2688]{2,1,0:T(8,128)(2,1)S(1)} collective-permute-done((bf16[2,128,2688]{2,1,0:T(8,128)(2,1)S(1)}, bf16[2,128,2688]{2,1,0:T(8,128)(2,1)S(1)}, u32[]{:S(2)}, u32[]{:S(2)}) %collective-permute-start) | collective-permute-done | bytes 1376288 | tf_op jit(solution)/shard_map/ppermute | solution.py:39
  54.4 4.2 pad_maximum_fusion
  58.6 3.5 gather_fusion
  62.1 2.2 bitcast_select_fusion.1
  64.4 0.7 all-gather.6.cloned.1.call-update
  65.2 0.7 all-gather.8.cloned.1.call-update
  65.9 1.5 collective-permute-start.3
  67.8 28.8 %collective-permute-done.2 = bf16[1344,512]{1,0:T(8,128)(2,1)} collective-permute-done((bf16[1344,512]{1,0:T(8,128)(2,1)S(1)}, bf16[1344,512]{1,0:T(8,128)(2,1)}, u32[]{:S(2)}, u32[]{:S(2)}) %collective-permute-start.2) | collective-permute-done | bytes 1376288 | tf_op jit(solution)/shard_map/ppermute | solution.py:24
  96.7 1.3 collective-permute-start.4
  98.1 1.0 multiply_cosine_fusion
  99.3 2.8 broadcast_in_dim.164
  102.1 1.2 constant_dynamic-update-slice_fusion.3
  103.3 2.6 constant_dynamic-update-slice_fusion.2
  105.8 47.4 %collective-permute-done.3 = bf16[1344,512]{1,0:T(8,128)(2,1)} collective-permute-done((bf16[1344,512]{1,0:T(8,128)(2,1)S(1)}, bf16[1344,512]{1,0:T(8,128)(2,1)}, u32[]{:S(2)}, u32[]{:S(2)}) %collective-permute-start.3) | collective-permute-done | bytes 1376288 | tf_op jit(solution)/shard_map/ppermute | solution.py:29
  153.3 2.6 constant_dynamic-update-slice_fusion.1
  155.8 60.5 %collective-permute-done.4 = bf16[1344,512]{1,0:T(8,128)(2,1)} collective-permute-done((bf16[1344,512]{1,0:T(8,128)(2,1)}, bf16[1344,512]{1,0:T(8,128)(2,1)}, u32[]{:S(2)}, u32[]{:S(2)}) %collective-permute-start.4) | collective-permute-done | bytes 1376288 | tf_op jit(solution)/shard_map/ppermute | solution.py:24
  216.3 2.5 constant_dynamic-update-slice_fusion
  218.8 3.9 fusion.6
  223.0 5.8 %multiply_reduce_fusion.1 = (f32[512,4]{0,1:T(4,128)S(1)}, f32[512,512]{0,1:T(8,128)S(1)}) fusion(bf16[5376,512]{1,0:T(8,128)(2,1)} %constant_dynamic-update-slice_fusion, bf16[512,5376]{1,0:T(8,128)(2,1)S(1)} %copy-done.1, f32[5376]{0:T(1024)S(1)} %copy-done.9, f32[512]{0:T(512)S(1)} %add_rsqrt_fusion.2), kind=kOutput, calls=%fused_computation.34 | convolution fusion | flops 2830104576 | bytes 12090368 | tf_op jit(solution)/shard_map/dot_general | solution.py:142
  229.3 16.6 %all-gather.6.cloned.1.call-done = bf16[5376,512]{1,0:T(8,128)(2,1)} async-done(((bf16[1344,512]{1,0:T(8,128)(2,1)}), bf16[5376,512]{1,0:T(8,128)(2,1)}) %all-gather.6.cloned.1.call-update) | async-done | bytes 5505040 | tf_op jit(solution)/shard_map/all_gather | solution.py:139
  245.9 7.3 %convolution_convert_fusion = bf16[512,512]{0,1:T(8,128)(2,1)S(1)} fusion(bf16[5376,512]{1,0:T(8,128)(2,1)} %all-gather.6.cloned.1.call-done, bf16[512,5376]{1,0:T(8,128)(2,1)} %all-gather.4.cloned.1.call-done, f32[5376]{0:T(1024)S(1)} %copy-done.9, f32[512]{0:T(512)S(1)} %add_rsqrt_fusion.2), kind=kOutput, calls=%fused_computation.31 | convolution fusion | flops 2829844480 | bytes 11557888 | tf_op jit(solution)/shard_map/dot_general | solution.py:142
  253.3 1.3 collective-permute-start.6
  254.6 1.5 collective-permute-start.5
  256.4 2.6 fusion.10
  259.0 55.0 %collective-permute-done.6 = bf16[512,1024]{0,1:T(8,128)(2,1)S(1)} collective-permute-done((bf16[512,1024]{0,1:T(8,128)(2,1)S(1)}, bf16[512,1024]{0,1:T(8,128)(2,1)S(1)}, u32[]{:S(2)}, u32[]{:S(2)}) %collective-permute-start.6) | collective-permute-done | bytes 1048608 | tf_op jit(solution)/shard_map/ppermute | solution.py:39
  314.0 117.6 %collective-permute-done.5 = bf16[512,1024]{0,1:T(8,128)(2,1)S(1)} collective-permute-done((bf16[512,1024]{0,1:T(8,128)(2,1)S(1)}, bf16[512,1024]{0,1:T(8,128)(2,1)S(1)}, u32[]{:S(2)}, u32[]{:S(2)}) %collective-permute-start.5) | collective-permute-done | bytes 1048608 | tf_op jit(solution)/shard_map/ppermute | solution.py:39
  431.6 9.2 %maximum_maximum_fusion = bf16[1536,1024]{0,1:T(8,128)(2,1)S(1)} fusion(bf16[512,512]{0,1:T(8,128)(2,1)S(1)} %convolution_convert_fusion, bf16[512,512]{0,1:T(8,128)(2,1)S(1)} %bitcast.52, bf16[512,1024]{0,1:T(8,128)(2,1)S(1)} %collective-permute-done.6, bf16[512,1024]{0,1:T(8,128)(2,1)S(1)} %collective-permute-done.5), kind=kLoop, calls=%fused_computation.15 | loop fusion | flops 12582912 | bytes 6291456 | tf_op jit(solution)/shard_map/concatenate | solution.py:205
  440.7 1.9 fusion.35
  442.7 60.0 %all-gather.8.cloned.1.call-done = bf16[5376,1024]{1,0:T(8,128)(2,1)} async-done(((bf16[1344,1024]{1,0:T(8,128)(2,1)}), bf16[5376,1024]{1,0:T(8,128)(2,1)}) %all-gather.8.cloned.1.call-update) | async-done | bytes 11010064 | tf_op jit(solution)/shard_map/all_gather | solution.py:137
  502.7 10.3 %convolution_bitcast_fusion = f32[64,8,8,128]{3,1,2,0:T(8,128)S(1)} fusion(bf16[5376,1024]{1,0:T(8,128)(2,1)} %all-gather.8.cloned.1.call-done, bf16[512,5376]{1,0:T(8,128)(2,1)} %all-gather.4.cloned.1.call-done, f32[5376]{0:T(1024)S(1)} %copy-done.9, f32[512]{0:T(512)S(1)} %add_rsqrt_fusion.2), kind=kOutput, calls=%fused_computation.28 | convolution fusion | flops 5648154624 | bytes 18635776 | tf_op jit(solution)/shard_map/dot_general | solution.py:142
  513.0 0.5 copy.42
  513.5 0.6 multiply_reduce_fusion
  514.4 0.9 multiply_multiply_fusion
  515.3 1.1 multiply_subtract_fusion
  516.4 0.6 fusion.11
  517.1 0.6 copy-done.3
  518.0 11.4 %fusion = (f32[4,2,512]{2,1,0:T(2,128)S(1)}, f32[4,1536,512,2]{2,1,3,0:T(8,128)}) fusion(pred[512,1536]{0,1:T(8,128)(4,1)S(1)} %copy-done.5, bf16[1536,4,128,1]{0,2,3,1:T(8,128)(2,1)S(1)} %bitcast.54, bf16[512,4,2,128]{3,0,2,1:T(8,128)(2,1)S(1)} %bitcast.55), kind=kOutput, calls=%fused_computation.4 | convolution fusion | flops 1623191552 | bytes 28590080 | tf_op jit(solution)/shard_map/while/body/eval_jaxpr/qgjd,kgd->gjqk/dot_general | solution.py:156
  529.4 10.7 %fusion.12 = bf16[512,4,2,128]{0,3,2,1:T(8,128)(2,1)S(1)} fusion(bf16[1536,4,128,1]{0,2,3,1:T(8,128)(2,1)S(1)} %bitcast.53, f32[4,1536,512,2]{2,1,3,0:T(8,128)} %get-tuple-element.57, pred[512,1536]{0,1:T(8,128)(4,1)S(1)} %copy-done.5, f32[512,4,2]{0,2,1:T(2,128)S(1)} %bitcast.57), kind=kOutput, calls=%fused_computation.23 | convolution fusion | flops 1624244224 | bytes 28590080 | tf_op jit(solution)/shard_map/while/body/eval_jaxpr/gjqk,kgd->qgjd/dot_general | solution.py:167
  540.1 1.3 copy.36
  (60 shorter events, 3.3 us)
Async XLA Ops:
  6.5 11.9 %copy-start = (bf16[512,2688]{1,0:T(8,128)(2,1)S(1)}, bf16[512,2688]{1,0:T(8,128)(2,1)}, u32[]{:S(2)}) copy-start(bf16[512,2688]{1,0:T(8,128)(2,1)} %param.11) | copy-start | bytes 8257540
  6.5 212.3 %all-gather.4.cloned.1.call-start = ((), (), s32[]{:S(2)}) async-start(), calls=%async_computation | async-start | bytes 8257536 | tf_op jit(solution)/shard_map/all_gather | solution.py:129
  15.2 31.2 %collective-permute-start.1 = (bf16[2,128,2688]{2,1,0:T(8,128)(2,1)}, bf16[2,128,2688]{2,1,0:T(8,128)(2,1)}, u32[]{:S(2)}, u32[]{:S(2)}) collective-permute-start(bf16[2,128,2688]{2,1,0:T(8,128)(2,1)} %broadcast_select_fusion), channel_id=1, source_target_pairs={{4,0},{8,4},{12,8},{5,1},{9,5},{13,9},{6,2},{10,6},{14,10},{7,3},{... | collective-permute-start | bytes 4128776 | tf_op jit(solution)/shard_map/ppermute | solution.py:39
  21.8 32.6 %collective-permute-start = (bf16[2,128,2688]{2,1,0:T(8,128)(2,1)S(1)}, bf16[2,128,2688]{2,1,0:T(8,128)(2,1)S(1)}, u32[]{:S(2)}, u32[]{:S(2)}) collective-permute-start(bf16[2,128,2688]{2,1,0:T(8,128)(2,1)S(1)} %broadcast_select_fusion.1), channel_id=1, source_target_pairs={{0,4},{4,8},{8,12},{1,5},{5,9},{9,13},{2,6},{6,10},{10,14},{3,7},{... | collective-permute-start | bytes 4128776 | tf_op jit(solution)/shard_map/ppermute | solution.py:39
  64.3 1.5 copy-start.4
  64.3 3.0 copy-start.6
  64.4 181.5 %all-gather.6.cloned.1.call-start = ((), (), s32[]{:S(2)}) async-start(), calls=%async_computation.1 | async-start | bytes 6881280 | tf_op jit(solution)/shard_map/all_gather | solution.py:139
  65.1 437.6 %all-gather.8.cloned.1.call-start = ((), (), s32[]{:S(2)}) async-start(), calls=%async_computation.2 | async-start | bytes 13762560 | tf_op jit(solution)/shard_map/all_gather | solution.py:137
  65.9 30.8 %collective-permute-start.2 = (bf16[1344,512]{1,0:T(8,128)(2,1)S(1)}, bf16[1344,512]{1,0:T(8,128)(2,1)}, u32[]{:S(2)}, u32[]{:S(2)}) collective-permute-start(bf16[1344,512]{1,0:T(8,128)(2,1)S(1)} %copy-done.4), channel_id=1, source_target_pairs={{0,4},{4,8},{8,12},{12,0},{1,5},{5,9},{9,13},{13,1},{2,6},{6,10},{... | collective-permute-start | bytes 4128776 | tf_op jit(solution)/shard_map/ppermute | solution.py:24
  65.9 87.3 %collective-permute-start.3 = (bf16[1344,512]{1,0:T(8,128)(2,1)S(1)}, bf16[1344,512]{1,0:T(8,128)(2,1)}, u32[]{:S(2)}, u32[]{:S(2)}) collective-permute-start(bf16[1344,512]{1,0:T(8,128)(2,1)S(1)} %copy-done.4), channel_id=1, source_target_pairs={{0,12},{4,0},{8,4},{12,8},{1,13},{5,1},{9,5},{13,9},{2,14},{6,2},{... | collective-permute-start | bytes 4128776 | tf_op jit(solution)/shard_map/ppermute | solution.py:29
  96.7 119.6 %collective-permute-start.4 = (bf16[1344,512]{1,0:T(8,128)(2,1)}, bf16[1344,512]{1,0:T(8,128)(2,1)}, u32[]{:S(2)}, u32[]{:S(2)}) collective-permute-start(bf16[1344,512]{1,0:T(8,128)(2,1)} %collective-permute-done.2), channel_id=1, source_target_pairs={{0,4},{4,8},{8,12},{12,0},{1,5},{5,9},{9,13},{13,1},{2,6},{6,10},{... | collective-permute-start | bytes 4128776 | tf_op jit(solution)/shard_map/ppermute | solution.py:24
  216.3 6.4 %copy-start.9 = (f32[5376]{0:T(1024)S(1)}, f32[5376]{0:T(1024)}, u32[]{:S(2)}) copy-start(f32[5376]{0:T(1024)} %param.12) | copy-start | bytes 64516
  218.8 4.2 copy-start.1
  223.0 5.9 %copy-start.7 = (f32[128]{0:T(128)S(1)}, f32[128]{0:T(128)}, u32[]{:S(2)}) copy-start(f32[128]{0:T(128)} %param.17) | copy-start | bytes 1540
  253.3 60.7 %collective-permute-start.6 = (bf16[512,1024]{0,1:T(8,128)(2,1)S(1)}, bf16[512,1024]{0,1:T(8,128)(2,1)S(1)}, u32[]{:S(2)}, u32[]{:S(2)}) collective-permute-start(bf16[512,1024]{0,1:T(8,128)(2,1)S(1)} %pad_maximum_fusion.1), channel_id=1, source_target_pairs={{0,4},{4,8},{8,12},{1,5},{5,9},{9,13},{2,6},{6,10},{10,14},{3,7},{... | collective-permute-start | bytes 3145736 | tf_op jit(solution)/shard_map/ppermute | solution.py:39
  254.6 177.0 %collective-permute-start.5 = (bf16[512,1024]{0,1:T(8,128)(2,1)S(1)}, bf16[512,1024]{0,1:T(8,128)(2,1)S(1)}, u32[]{:S(2)}, u32[]{:S(2)}) collective-permute-start(bf16[512,1024]{0,1:T(8,128)(2,1)S(1)} %pad_maximum_fusion.1), channel_id=1, source_target_pairs={{0,8},{4,12},{1,9},{5,13},{2,10},{6,14},{3,11},{7,15},{16,24},{20,... | collective-permute-start | bytes 3145736 | tf_op jit(solution)/shard_map/ppermute | solution.py:39
  513.0 1.4 copy-start.8
  516.4 1.4 copy-start.3
  516.4 1.6 copy-start.5
  518.0 11.4 %copy-start.2 = (bf16[1536,512]{0,1:T(8,128)(2,1)S(1)}, bf16[1536,512]{0,1:T(8,128)(2,1)}, u32[]{:S(2)}) copy-start(bf16[1536,512]{0,1:T(8,128)(2,1)} %get-tuple-element.40) | copy-start | bytes 4718596
Sparse Core Ops, SparseCore 0:
  64.5 18.4 all-gather.3
  84.6 161.2 all-gather.5
  247.4 255.1 all-gather.7
